TPU v7x, 32 devices: a whole 2x2x4 slice. The times are simulated.
32 devices in a mesh: fsdp: 32 (over z, y, x, core).
Axes of the slice: x: 2, y: 2, z: 4, core: 2. Of those that a mesh axis runs over, the one named last changes fastest.
Arguments:
- tokens: bfloat16 [65536, 768], P('fsdp'), may hold values from -6 to 6
- cotangent: bfloat16 [65536, 768], P('fsdp'), may hold values from -6 to 6
- segments: int32 [65536], P('fsdp'), may hold values from 0 to 1, as said below
- positions: int32 [65536], P('fsdp'), may hold values from 0 to 1999, as said below
- qkv_weight: float32 [768, 2304], P('fsdp'), may hold values from -0.21875 to 0.21875
- qkv_first: float32 [768, 2304], P('fsdp'), may hold values from -160 to 160
- qkv_second: float32 [768, 2304], P('fsdp'), may hold values from 1310 to 5461
- out_weight: float32 [768, 768], P('fsdp'), may hold values from -0.625 to 0.625
- out_first: float32 [768, 768], P('fsdp'), may hold values from -160 to 160
- out_second: float32 [768, 768], P('fsdp'), may hold values from 1310 to 5461
- in_weight: float32 [768, 2304], P('fsdp'), may hold values from -0.21875 to 0.21875
- in_first: float32 [768, 2304], P('fsdp'), may hold values from -160 to 160
- in_second: float32 [768, 2304], P('fsdp'), may hold values from 1310 to 5461
- down_weight: float32 [1152, 768], P('fsdp'), may hold values from -0.375 to 0.375
- down_first: float32 [1152, 768], P('fsdp'), may hold values from -160 to 160
- down_second: float32 [1152, 768], P('fsdp'), may hold values from 1310 to 5461
- norm_gains: float32 [2, 768], P(None, 'fsdp'), may hold values from 0.5 to 1.5
- gains_first: float32 [2, 768], P(None, 'fsdp'), may hold values from -160 to 160
- gains_second: float32 [2, 768], P(None, 'fsdp'), may hold values from 1310 to 5461
Outputs:
- activations: bfloat16 [65536, 768], P('fsdp')
- input_grad: float32 [65536, 768], P('fsdp')
- qkv_grad: float32 [768, 2304], P('fsdp')
- qkv_new: float32 [768, 2304], P('fsdp')
- qkv_first_new: float32 [768, 2304], P('fsdp')
- qkv_second_new: float32 [768, 2304], P('fsdp')
- out_grad: float32 [768, 768], P('fsdp')
- out_new: float32 [768, 768], P('fsdp')
- out_first_new: float32 [768, 768], P('fsdp')
- out_second_new: float32 [768, 768], P('fsdp')
- in_grad: float32 [768, 2304], P('fsdp')
- in_new: float32 [768, 2304], P('fsdp')
- in_first_new: float32 [768, 2304], P('fsdp')
- in_second_new: float32 [768, 2304], P('fsdp')
- down_grad: float32 [1152, 768], P('fsdp')
- down_new: float32 [1152, 768], P('fsdp')
- down_first_new: float32 [1152, 768], P('fsdp')
- down_second_new: float32 [1152, 768], P('fsdp')
- gains_grad: float32 [2, 768], P(None, 'fsdp')
- gains_delta: float32 [2, 768], P(None, 'fsdp')
- gains_first_new: float32 [2, 768], P(None, 'fsdp')
- gains_second_new: float32 [2, 768], P(None, 'fsdp')
Inputs may be any that keep to these rules, and one draw needn't show every extreme that they name: `segments`: documents lie end to end over all 65536 tokens; the segment number is 0 on the first document and changes between 0 and 1 from each document to the next. Each document is 200 to 2000 tokens long, the last cut at the end, and both lengths occur. A document may run across packed sequences. `positions`: place of each token in its document counted from 0; it grows by one from token to token inside a document and starts again at 0 where the segment number changes.
All inputs are finite; a program needn't handle non-finite values.
Results may differ from a plain program's by a relative error of at most 0.019.
Values may be sent and summed in bfloat16 or wider, within the bound.
A program may use at most 256 MiB of HBM per device.

v0:
```python
import jax
import jax.numpy as jnp
from jax import lax
from jax.sharding import PartitionSpec as P

D = 768
HEADS = 12
HEAD = 64
FF = 1152
SEQ = 512
BLK = 128
STEP = 10
NORM_EPS = 1e-05
BETA_ONE = 0.9
BETA_TWO = 0.98
ADAM_EPS = 1e-06
LEARN_RATE = 0.1
WEIGHT_DECAY = 0.01
ROPE_BASE = 10000.0
MASKED = -1e30


def layer_norm(values, norm_gain):
    center = values - jnp.mean(values, axis=-1, keepdims=True)
    spread = jnp.mean(center * center, axis=-1, keepdims=True)
    return center * lax.rsqrt(spread + NORM_EPS) * norm_gain


def rotate(values, cosine, sine):
    half_dim = values.shape[-1] // 2
    turned = jnp.concatenate([-values[..., half_dim:], values[..., :half_dim]], axis=-1)
    return values * cosine + turned * sine


def rope_tables(places):
    half_dim = HEAD // 2
    frequency = ROPE_BASE ** (-(jnp.arange(half_dim).astype(jnp.float32) * 2.0 / HEAD))
    angles = places.astype(jnp.float32)[:, None] * frequency[None, :]
    angles = jnp.concatenate([angles, angles], axis=-1)
    return (jnp.cos(angles)[:, None, :], jnp.sin(angles)[:, None, :])


def widen(blocked):
    before = jnp.roll(blocked, 1, axis=0)
    after = jnp.roll(blocked, -1, axis=0)
    return jnp.concatenate([before, blocked, after], axis=1)


def fold_wide(wide):
    block_width = wide.shape[1] // 3
    middle = wide[:, block_width : 2 * block_width]
    return (
        middle
        + jnp.roll(wide[:, :block_width], -1, axis=0)
        + jnp.roll(wide[:, 2 * block_width :], 1, axis=0)
    )


def window_mask(seq_segs, block_width):
    row_count = seq_segs.shape[0]
    block_count = row_count // block_width
    starts = jnp.arange(block_count)[:, None, None] * block_width
    query_at = starts + jnp.arange(block_width)[None, :, None]
    key_at = starts - block_width + jnp.arange(3 * block_width)[None, None, :]
    seg_blocks = seq_segs.reshape(block_count, block_width)
    seg_wide = widen(seg_blocks)
    in_window = jnp.abs(query_at - key_at) <= block_width // 2
    inside = (key_at >= 0) & (key_at < row_count)
    same_doc = seg_blocks[:, :, None] == seg_wide[:, None, :]
    return in_window & inside & same_doc


def block_scores(query_heads, key_heads, seq_segs):
    block_count = query_heads.shape[0] // BLK
    query_blocks = query_heads.reshape(block_count, BLK, HEADS, HEAD)
    key_wide = widen(key_heads.reshape(block_count, BLK, HEADS, HEAD))
    scores = jnp.einsum(
        "bqhe,bkhe->bhqk", query_blocks, key_wide, preferred_element_type=jnp.float32
    ) * HEAD ** (-0.5)
    allowed = window_mask(seq_segs, BLK)[:, None]
    return (jnp.where(allowed, scores, MASKED), query_blocks, key_wide)


def attend(seq_items):
    query_heads, key_heads, value_heads, seq_segs = seq_items
    scores, query_blocks, key_wide = block_scores(query_heads, key_heads, seq_segs)
    row_top = jnp.max(scores, axis=-1, keepdims=True)
    exp_scores = jnp.exp(scores - row_top)
    row_total = jnp.sum(exp_scores, axis=-1, keepdims=True)
    prob_low = (exp_scores / row_total).astype(jnp.bfloat16)
    value_wide = widen(value_heads.reshape(query_blocks.shape))
    attended = jnp.einsum(
        "bhqk,bkhe->bqhe", prob_low, value_wide, preferred_element_type=jnp.float32
    )
    return (attended.reshape(value_heads.shape).astype(jnp.bfloat16), row_top + jnp.log(row_total))


def attend_back(seq_items):
    query_heads, key_heads, value_heads, grad_heads, log_total, seq_segs = seq_items
    scores, query_blocks, key_wide = block_scores(query_heads, key_heads, seq_segs)
    value_wide = widen(value_heads.reshape(query_blocks.shape))
    grad_blocks = grad_heads.reshape(query_blocks.shape)
    attn_prob = jnp.exp(scores - log_total)
    prob_low = attn_prob.astype(jnp.bfloat16)
    grad_value_wide = jnp.einsum(
        "bhqk,bqhe->bkhe", prob_low, grad_blocks, preferred_element_type=jnp.float32
    )
    grad_prob = jnp.einsum(
        "bqhe,bkhe->bhqk", grad_blocks, value_wide, preferred_element_type=jnp.float32
    )
    inner = jnp.sum(attn_prob * grad_prob, axis=-1, keepdims=True)
    grad_scores = (attn_prob * (grad_prob - inner)).astype(jnp.bfloat16)
    scale_factor = HEAD ** (-0.5)
    grad_query = (
        jnp.einsum("bhqk,bkhe->bqhe", grad_scores, key_wide, preferred_element_type=jnp.float32)
        * scale_factor
    )
    grad_key_wide = (
        jnp.einsum("bhqk,bqhe->bkhe", grad_scores, query_blocks, preferred_element_type=jnp.float32)
        * scale_factor
    )
    head_shape = query_heads.shape
    return (
        grad_query.reshape(head_shape),
        fold_wide(grad_key_wide).reshape(head_shape),
        fold_wide(grad_value_wide).reshape(head_shape),
    )


def split_seqs(array, seq_count):
    return array.reshape((seq_count, SEQ) + array.shape[1:])


def adam_step(master, weight_grad, moment_one, moment_two):
    first_new = BETA_ONE * moment_one + (1.0 - BETA_ONE) * weight_grad
    second_new = BETA_TWO * moment_two + (1.0 - BETA_TWO) * weight_grad * weight_grad
    first_hat = first_new / (1.0 - BETA_ONE**STEP)
    second_hat = second_new / (1.0 - BETA_TWO**STEP)
    master_new = master - LEARN_RATE * (
        first_hat / (jnp.sqrt(second_hat) + ADAM_EPS) + WEIGHT_DECAY * master
    )
    return (weight_grad, master_new, first_new, second_new)


def geglu(gate_up):
    return jax.nn.gelu(gate_up[:, :FF], approximate=False) * gate_up[:, FF:]


def shards(
    tokens,
    cotangent,
    segments,
    positions,
    qkv_weight,
    qkv_first,
    qkv_second,
    out_weight,
    out_first,
    out_second,
    in_weight,
    in_first,
    in_second,
    down_weight,
    down_first,
    down_second,
    norm_gains,
    gains_first,
    gains_second,
):
    masters = (qkv_weight, out_weight, in_weight, down_weight, norm_gains)
    rounded = tuple((master.astype(jnp.bfloat16) for master in masters))
    gathered = (
        lax.all_gather(rounded[0], "fsdp", axis=0, tiled=True),
        lax.all_gather(rounded[1], "fsdp", axis=0, tiled=True),
        lax.all_gather(rounded[2], "fsdp", axis=0, tiled=True),
        lax.all_gather(rounded[3], "fsdp", axis=0, tiled=True),
        lax.all_gather(rounded[4], "fsdp", axis=1, tiled=True),
    )
    qkv_low, out_low, in_low, down_low, gains_low = gathered
    gains_full = gains_low.astype(jnp.float32)
    row_count = tokens.shape[0]
    seq_count = row_count // SEQ
    hidden_in = tokens.astype(jnp.float32)
    normed, norm_back_one = jax.vjp(layer_norm, hidden_in, gains_full[0])
    normed_low = normed.astype(jnp.bfloat16)
    qkv_mixed = jnp.dot(normed_low, qkv_low, preferred_element_type=jnp.float32)
    cosine, sine = rope_tables(positions)
    query_heads = rotate(qkv_mixed[:, :D].reshape(row_count, HEADS, HEAD), cosine, sine).astype(
        jnp.bfloat16
    )
    key_heads = rotate(
        qkv_mixed[:, D : 2 * D].reshape(row_count, HEADS, HEAD), cosine, sine
    ).astype(jnp.bfloat16)
    value_heads = qkv_mixed[:, 2 * D :].reshape(row_count, HEADS, HEAD).astype(jnp.bfloat16)
    seq_queries = split_seqs(query_heads, seq_count)
    seq_keys = split_seqs(key_heads, seq_count)
    seq_values = split_seqs(value_heads, seq_count)
    seq_segments = split_seqs(segments, seq_count)
    attended, log_total = lax.map(attend, (seq_queries, seq_keys, seq_values, seq_segments))
    attended_low = attended.reshape(row_count, D)
    residual = hidden_in + jnp.dot(attended_low, out_low, preferred_element_type=jnp.float32)
    normed_two, norm_back_two = jax.vjp(layer_norm, residual, gains_full[1])
    normed_two_low = normed_two.astype(jnp.bfloat16)
    gate_up = jnp.dot(normed_two_low, in_low, preferred_element_type=jnp.float32)
    active, geglu_back = jax.vjp(geglu, gate_up)
    active_low = active.astype(jnp.bfloat16)
    output = residual + jnp.dot(active_low, down_low, preferred_element_type=jnp.float32)
    activations = output.astype(jnp.bfloat16)
    gathered_back = (
        lax.all_gather(rounded[0], "fsdp", axis=0, tiled=True),
        lax.all_gather(rounded[1], "fsdp", axis=0, tiled=True),
        lax.all_gather(rounded[2], "fsdp", axis=0, tiled=True),
        lax.all_gather(rounded[3], "fsdp", axis=0, tiled=True),
        lax.all_gather(rounded[4], "fsdp", axis=1, tiled=True),
    )
    qkv_low, out_low, in_low, down_low, gains_low = gathered_back
    grad_down = jnp.dot(active_low.T, cotangent, preferred_element_type=jnp.float32)
    grad_active = jnp.dot(cotangent, down_low.T, preferred_element_type=jnp.float32)
    grad_gate_up = geglu_back(grad_active)[0].astype(jnp.bfloat16)
    grad_in = jnp.dot(normed_two_low.T, grad_gate_up, preferred_element_type=jnp.float32)
    grad_normed_two = jnp.dot(grad_gate_up, in_low.T, preferred_element_type=jnp.float32)
    grad_resid_norm, gain_two_grad = norm_back_two(grad_normed_two)
    grad_residual = cotangent.astype(jnp.float32) + grad_resid_norm
    grad_residual_low = grad_residual.astype(jnp.bfloat16)
    grad_outw = jnp.dot(attended_low.T, grad_residual_low, preferred_element_type=jnp.float32)
    grad_attended = jnp.dot(
        grad_residual_low, out_low.T, preferred_element_type=jnp.float32
    ).astype(jnp.bfloat16)
    seq_grad_heads = split_seqs(grad_attended.reshape(row_count, HEADS, HEAD), seq_count)
    grad_queries, grad_keys, grad_values = lax.map(
        attend_back, (seq_queries, seq_keys, seq_values, seq_grad_heads, log_total, seq_segments)
    )
    grad_queries = rotate(grad_queries.reshape(row_count, HEADS, HEAD), cosine, -sine)
    grad_keys = rotate(grad_keys.reshape(row_count, HEADS, HEAD), cosine, -sine)
    grad_mixed = jnp.concatenate(
        [
            grad_queries.reshape(row_count, D),
            grad_keys.reshape(row_count, D),
            grad_values.reshape(row_count, D),
        ],
        axis=1,
    ).astype(jnp.bfloat16)
    grad_qkv = jnp.dot(normed_low.T, grad_mixed, preferred_element_type=jnp.float32)
    grad_normed = jnp.dot(grad_mixed, qkv_low.T, preferred_element_type=jnp.float32)
    grad_input_norm, gain_one_grad = norm_back_one(grad_normed)
    input_grad = grad_residual + grad_input_norm
    gain_pair_grad = jnp.stack([gain_one_grad, gain_two_grad])
    owned_qkv, owned_out, owned_in, owned_down, owned_gain = (
        lax.psum_scatter(grad_qkv, "fsdp", scatter_dimension=0, tiled=True),
        lax.psum_scatter(grad_outw, "fsdp", scatter_dimension=0, tiled=True),
        lax.psum_scatter(grad_in, "fsdp", scatter_dimension=0, tiled=True),
        lax.psum_scatter(grad_down, "fsdp", scatter_dimension=0, tiled=True),
        lax.psum_scatter(gain_pair_grad, "fsdp", scatter_dimension=1, tiled=True),
    )
    qkv_state = adam_step(qkv_weight, owned_qkv, qkv_first, qkv_second)
    out_state = adam_step(out_weight, owned_out, out_first, out_second)
    in_state = adam_step(in_weight, owned_in, in_first, in_second)
    down_state = adam_step(down_weight, owned_down, down_first, down_second)
    gains_state = adam_step(norm_gains, owned_gain, gains_first, gains_second)
    gains_delta = gains_state[1] - norm_gains
    return (
        activations,
        input_grad,
        qkv_state[0],
        qkv_state[1],
        qkv_state[2],
        qkv_state[3],
        out_state[0],
        out_state[1],
        out_state[2],
        out_state[3],
        in_state[0],
        in_state[1],
        in_state[2],
        in_state[3],
        down_state[0],
        down_state[1],
        down_state[2],
        down_state[3],
        gains_state[0],
        gains_delta,
        gains_state[2],
        gains_state[3],
    )


def solution(mesh):
    return jax.shard_map(
        shards,
        mesh=mesh,
        in_specs=(
            P("fsdp", None),
            P("fsdp", None),
            P("fsdp"),
            P("fsdp"),
            P("fsdp", None),
            P("fsdp", None),
            P("fsdp", None),
            P("fsdp", None),
            P("fsdp", None),
            P("fsdp", None),
            P("fsdp", None),
            P("fsdp", None),
            P("fsdp", None),
            P("fsdp", None),
            P("fsdp", None),
            P("fsdp", None),
            P(None, "fsdp"),
            P(None, "fsdp"),
            P(None, "fsdp"),
        ),
        out_specs=(
            P("fsdp", None),
            P("fsdp", None),
            P("fsdp", None),
            P("fsdp", None),
            P("fsdp", None),
            P("fsdp", None),
            P("fsdp", None),
            P("fsdp", None),
            P("fsdp", None),
            P("fsdp", None),
            P("fsdp", None),
            P("fsdp", None),
            P("fsdp", None),
            P("fsdp", None),
            P("fsdp", None),
            P("fsdp", None),
            P("fsdp", None),
            P("fsdp", None),
            P(None, "fsdp"),
            P(None, "fsdp"),
            P(None, "fsdp"),
            P(None, "fsdp"),
        ),
        check_vma=False,
    )
```

profile of v0, /device:TPU:0, one launch (start us, length us, event | category | flops | bytes accessed | tf_op | source)
XLA Modules:
  0.0 1512.9 jit_solution(8953548538941148751)
XLA Ops:
  18.5 43.1 %all-gather = bf16[32,24,2]{1,2,0:T(2,128)(2,1)S(1)} all-gather(bf16[1,24,2]{1,2,0:T(2,128)(2,1)S(1)} %convert_bitcast_fusion.1), channel_id=1, replica_groups=mesh['fsdp'=32] {'fsdp'}, dimensions={0}, use_global_device_ids=true | all-gather | bytes 3168 | tf_op jit(solution)/shard_map/all_gather | solution.py:177
  75.7 57.1 %all-gather.7.cloned.1.call-done = bf16[768,2304]{1,0:T(8,128)(2,1)} async-done(((bf16[24,2304]{1,0:T(8,128)(2,1)}), bf16[768,2304]{1,0:T(8,128)(2,1)}) %all-gather.7.cloned.1.call-update) | async-done | bytes 3538960 | tf_op jit(solution)/shard_map/all_gather | solution.py:173
  132.8 13.6 fusion.103
  224.1 10.3 fusion.94
  250.9 250.1 %while.30 = (s32[]{:T(128)}, bf16[4,512,12,64]{1,3,2,0:T(8,128)(2,1)}, f32[4,4,12,128,1]{3,2,1,4,0:T(8,128)}, bf16[4,512,12,64]{1,3,2,0:T(8,128)(2,1)S(1)}, s32[...) while((s32[]{:T(128)}, ...), condition=%wide.region_5.6_spmd, body=%wide.region_2.5_spmd.sunk | while | flops 657465344 | bytes 106623328 | solution.py:199
  518.7 11.3 fusion.121
  530.0 26.2 %fusion.98 = (f32[2048,1152]{1,0:T(8,128)}, f32[2048,1152]{1,0:T(8,128)}, f32[2048,1152]{1,0:T(8,128)}) fusion(f32[2048,2304]{1,0:T(8,128)S(1)} %fusion.121, bf16[2048,768]{1,0:T(8,128)(2,1)S(1)} %copy-done.19, bf16[1152,768]{1,0:T(8,128)(2,1)S(1)} %copy-done.25), kind=kOutput, calls=%fused_computation.188 | convolution fusion | flops 3777232896 | bytes 42663936 | tf_op jit(solution)/shard_map/dot_general | solution.py:218
  556.2 14.6 multiply_add_fusion
  570.7 16.2 %multiply_reduce_fusion.1 = (f32[768]{0:T(1024)}, f32[2048]{0:T(1024)S(1)}, f32[2048,768]{0,1:T(8,128)}) fusion(f32[2048,768]{0,1:T(8,128)} %copy-done.10, f32[2048]{0:T(1024)S(1)} %fusion.115, f32[2048]{0:T(1024)S(1)} %broadcast_multiply_fusion.2, f32[768]{0:T(1024)S(1)} %copy-done.41, bf16[768,2304]{1,0:T(8,128)(2,1)} %all-gather.11.cloned.1.call-done, ...), kind=kOutput, calls=%fused_computation.173 | convolution fusion | flops 7268201472 | bytes 35026944 | tf_op jit(solution)/shard_map/dot_general | solution.py:221
  621.2 19.0 %fusion.99 = f32[768,2304]{1,0:T(8,128)} fusion(f32[2048,1152]{1,0:T(8,128)} %get-tuple-element.515, f32[2048,1152]{1,0:T(8,128)} %get-tuple-element.463, f32[2048,768]{0,1:T(8,128)} %copy-done.10, f32[768]{0:T(1024)S(1)} %copy-done.41, f32[2048]{0:T(1024)S(1)} %fusion.115, f32[2048]{0:T(1024)S(1)} %broadcast_multiply_fusion.2), kind=kOutput, calls=%fused_computation.189 | convolution fusion | flops 7263485952 | bytes 32263168 | tf_op jit(solution)/shard_map/dot_general | solution.py:220
  642.0 588.1 %while.31 = (s32[]{:T(128)}, f32[4,512,12,64]{1,0,3,2:T(4,128)}, f32[4,512,12,64]{1,0,3,2:T(4,128)}, bf16[4,512,12,64]{1,3,2,0:T(8,128)(2,1)}, bf16[4,512,12,64]...) while((s32[]{:T(128)}, f32[4,512,12,64]{1,0,3,2:T(4,128)}, ...), condition=%wide.region_12.13_spmd, body=%wide.region_10.12_spmd.sunk | while | flops 1587027968 | bytes 218263584 | solution.py:230
  719.8 31.3 %dynamic_update_slice.45 = f32[4,512,12,64]{1,0,3,2:T(4,128)} dynamic-update-slice(f32[4,512,12,64]{1,0,3,2:T(4,128)} %get-tuple-element.790, f32[1,512,12,64]{1,0,3,2:T(1,128)} %bitcast.205, s32[]{:T(128)} %get-tuple-element.788, s32[]{:T(128)} %constant.218.clone.1..sunk.1, s32[]{:T(128)} %constant.218.clone.1..sunk.1, s32[]{:T(128)} %constant.218.clone.1..sunk.1) | dynamic-update-slice | bytes 3145732 | tf_op jit(solution)/shard_map/while/body/jit(dynamic_update_index_in_dim)/dynamic_update_slice | solution.py:230
  758.4 31.2 %dynamic_update_slice.44 = f32[4,512,12,64]{1,0,3,2:T(4,128)} dynamic-update-slice(f32[4,512,12,64]{1,0,3,2:T(4,128)} %get-tuple-element.789, f32[1,512,12,64]{1,0,3,2:T(1,128)} %bitcast.204, s32[]{:T(128)} %get-tuple-element.788, s32[]{:T(128)} %constant.218.clone.1..sunk.1, s32[]{:T(128)} %constant.218.clone.1..sunk.1, s32[]{:T(128)} %constant.218.clone.1..sunk.1) | dynamic-update-slice | bytes 3145732 | tf_op jit(solution)/shard_map/while/body/jit(dynamic_update_index_in_dim)/dynamic_update_slice | solution.py:230
  866.9 31.0 %dynamic_update_slice.45 = f32[4,512,12,64]{1,0,3,2:T(4,128)} dynamic-update-slice(f32[4,512,12,64]{1,0,3,2:T(4,128)} %get-tuple-element.790, f32[1,512,12,64]{1,0,3,2:T(1,128)} %bitcast.205, s32[]{:T(128)} %get-tuple-element.788, s32[]{:T(128)} %constant.218.clone.1..sunk.1, s32[]{:T(128)} %constant.218.clone.1..sunk.1, s32[]{:T(128)} %constant.218.clone.1..sunk.1) | dynamic-update-slice | bytes 3145732 | tf_op jit(solution)/shard_map/while/body/jit(dynamic_update_index_in_dim)/dynamic_update_slice | solution.py:230
  905.3 31.0 %dynamic_update_slice.44 = f32[4,512,12,64]{1,0,3,2:T(4,128)} dynamic-update-slice(f32[4,512,12,64]{1,0,3,2:T(4,128)} %get-tuple-element.789, f32[1,512,12,64]{1,0,3,2:T(1,128)} %bitcast.204, s32[]{:T(128)} %get-tuple-element.788, s32[]{:T(128)} %constant.218.clone.1..sunk.1, s32[]{:T(128)} %constant.218.clone.1..sunk.1, s32[]{:T(128)} %constant.218.clone.1..sunk.1) | dynamic-update-slice | bytes 3145732 | tf_op jit(solution)/shard_map/while/body/jit(dynamic_update_index_in_dim)/dynamic_update_slice | solution.py:230
  1013.7 31.0 %dynamic_update_slice.45 = f32[4,512,12,64]{1,0,3,2:T(4,128)} dynamic-update-slice(f32[4,512,12,64]{1,0,3,2:T(4,128)} %get-tuple-element.790, f32[1,512,12,64]{1,0,3,2:T(1,128)} %bitcast.205, s32[]{:T(128)} %get-tuple-element.788, s32[]{:T(128)} %constant.218.clone.1..sunk.1, s32[]{:T(128)} %constant.218.clone.1..sunk.1, s32[]{:T(128)} %constant.218.clone.1..sunk.1) | dynamic-update-slice | bytes 3145732 | tf_op jit(solution)/shard_map/while/body/jit(dynamic_update_index_in_dim)/dynamic_update_slice | solution.py:230
  1052.1 31.0 %dynamic_update_slice.44 = f32[4,512,12,64]{1,0,3,2:T(4,128)} dynamic-update-slice(f32[4,512,12,64]{1,0,3,2:T(4,128)} %get-tuple-element.789, f32[1,512,12,64]{1,0,3,2:T(1,128)} %bitcast.204, s32[]{:T(128)} %get-tuple-element.788, s32[]{:T(128)} %constant.218.clone.1..sunk.1, s32[]{:T(128)} %constant.218.clone.1..sunk.1, s32[]{:T(128)} %constant.218.clone.1..sunk.1) | dynamic-update-slice | bytes 3145732 | tf_op jit(solution)/shard_map/while/body/jit(dynamic_update_index_in_dim)/dynamic_update_slice | solution.py:230
  1160.4 31.0 %dynamic_update_slice.45 = f32[4,512,12,64]{1,0,3,2:T(4,128)} dynamic-update-slice(f32[4,512,12,64]{1,0,3,2:T(4,128)} %get-tuple-element.790, f32[1,512,12,64]{1,0,3,2:T(1,128)} %bitcast.205, s32[]{:T(128)} %get-tuple-element.788, s32[]{:T(128)} %constant.218.clone.1..sunk.1, s32[]{:T(128)} %constant.218.clone.1..sunk.1, s32[]{:T(128)} %constant.218.clone.1..sunk.1) | dynamic-update-slice | bytes 3145732 | tf_op jit(solution)/shard_map/while/body/jit(dynamic_update_index_in_dim)/dynamic_update_slice | solution.py:230
  1198.7 31.0 %dynamic_update_slice.44 = f32[4,512,12,64]{1,0,3,2:T(4,128)} dynamic-update-slice(f32[4,512,12,64]{1,0,3,2:T(4,128)} %get-tuple-element.789, f32[1,512,12,64]{1,0,3,2:T(1,128)} %bitcast.204, s32[]{:T(128)} %get-tuple-element.788, s32[]{:T(128)} %constant.218.clone.1..sunk.1, s32[]{:T(128)} %constant.218.clone.1..sunk.1, s32[]{:T(128)} %constant.218.clone.1..sunk.1) | dynamic-update-slice | bytes 3145732 | tf_op jit(solution)/shard_map/while/body/jit(dynamic_update_index_in_dim)/dynamic_update_slice | solution.py:230
  1291.3 14.2 fusion.96
  1314.7 89.5 %fusion = f32[40,768]{1,0:T(8,128)S(1)} fusion(f32[1152,768]{1,0:T(8,128)} %fusion.138), kind=kCustom, calls=%all-reduce-scatter | all-reduce-scatter fusion | flops 983041 | bytes 3661824
  1410.0 11.3 fusion.86
  1428.5 38.5 %all-reduce.3 = f32[2,768]{1,0:T(2,128)S(1)} all-reduce(f32[2,768]{1,0:T(2,128)S(1)} %pad_maximum_fusion.5), channel_id=6, replica_groups=mesh['fsdp'=32] {'fsdp'}, use_global_device_ids=true, to_apply=%region_21.22.clone | all-reduce | flops 1536 | bytes 12288
  1467.0 10.8 add_convert_fusion.1
  (621 shorter events, 871.7 us)
Async XLA Ops:
  7.2 64.9 %all-gather.13.cloned.1.call-start = ((), (), s32[]{:S(2)}) async-start(), calls=%async_computation.9 | async-start | bytes 2027520 | tf_op jit(solution)/shard_map/all_gather | solution.py:176
  8.8 123.9 %all-gather.7.cloned.1.call-start = ((), (), s32[]{:S(2)}) async-start(), calls=%async_computation.3 | async-start | bytes 3649536 | tf_op jit(solution)/shard_map/all_gather | solution.py:173
  10.5 498.7 %all-gather.9.cloned.1.call-start = ((), (), s32[]{:S(2)}) async-start(), calls=%async_computation.4 | async-start | bytes 1216512 | tf_op jit(solution)/shard_map/all_gather | solution.py:174
  12.0 506.6 %all-gather.11.cloned.1.call-start = ((), (), s32[]{:S(2)}) async-start(), calls=%async_computation.5 | async-start | bytes 3649536 | tf_op jit(solution)/shard_map/all_gather | solution.py:175
  13.7 1486.1 %reduce-scatter.9.cloned.1.call-start = ((), (), s32[]{:S(2)}) async-start(), calls=%async_computation.7 | async-start | bytes 2433024 | tf_op jit(solution)/shard_map/reduce_scatter | solution.py:250
  13.8 48.7 %copy-start.45 = (f32[32]{0:T(128)}, f32[32]{0:T(128)S(1)}, u32[]{:S(2)}) copy-start(f32[32]{0:T(128)S(1)} %negate_power_fusion) | copy-start | bytes 388
  13.9 48.6 %copy-start.42 = (s32[2048]{0:T(1024)S(1)}, s32[2048]{0:T(1024)}, u32[]{:S(2)}) copy-start(s32[2048]{0:T(1024)} %param.26) | copy-start | bytes 24580
  13.9 53.4 %copy-start.43 = (s32[2048]{0:T(1024)S(1)}, s32[2048]{0:T(1024)}, u32[]{:S(2)}) copy-start(s32[2048]{0:T(1024)} %param.25) | copy-start | bytes 24580
  17.1 115.7 %copy-start.5 = (bf16[2048,768]{0,1:T(8,128)(2,1)}, bf16[2048,768]{0,1:T(8,128)(2,1)S(1)}, u32[]{:S(2)}) copy-start(bf16[2048,768]{0,1:T(8,128)(2,1)S(1)} %copy.171) | copy-start | bytes 9437188
  17.6 115.2 %copy-start.29 = (f32[2048]{0:T(1024)}, f32[2048]{0:T(1024)S(1)}, u32[]{:S(2)}) copy-start(f32[2048]{0:T(1024)S(1)} %broadcast_multiply_fusion.3) | copy-start | bytes 24580
  18.5 43.1 %copy-start.35 = (f32[2048]{0:T(1024)}, f32[2048]{0:T(1024)S(1)}, u32[]{:S(2)}) copy-start(f32[2048]{0:T(1024)S(1)} %fusion.85) | copy-start | bytes 24580
  18.5 127.9 %copy-start.31 = (f32[2048]{0:T(1024)}, f32[2048]{0:T(1024)S(1)}, u32[]{:S(2)}) copy-start(f32[2048]{0:T(1024)S(1)} %fusion.114) | copy-start | bytes 24580
  62.5 83.9 %copy-start.39 = (f32[768]{0:T(1024)}, f32[768]{0:T(1024)S(1)}, u32[]{:S(2)}) copy-start(f32[768]{0:T(1024)S(1)} %get-tuple-element.409) | copy-start | bytes 9220
  62.5 83.9 %copy-start.37 = (f32[2048]{0:T(1024)}, f32[2048]{0:T(1024)S(1)}, u32[]{:S(2)}) copy-start(f32[2048]{0:T(1024)S(1)} %convert_element_type.114) | copy-start | bytes 24580
  601.0 900.5 %reduce-scatter.11.cloned.1.call-start = ((), (), s32[]{:S(2)}) async-start(), calls=%async_computation.8 | async-start | bytes 7299072 | tf_op jit(solution)/shard_map/reduce_scatter | solution.py:251
  640.2 863.4 %reduce-scatter.7.cloned.1.call-start = ((), (), s32[]{:S(2)}) async-start(), calls=%async_computation.6 | async-start | bytes 7299072 | tf_op jit(solution)/shard_map/reduce_scatter | solution.py:249
  717.1 33.9 %copy-start.14 = (bf16[1,128,12,64]{1,3,2,0:T(8,128)(2,1)S(1)}, bf16[1,128,12,64]{1,3,2,0:T(8,128)(2,1)}, u32[]{:S(2)}) copy-start(bf16[1,128,12,64]{1,3,2,0:T(8,128)(2,1)} %copy-done.13) | copy-start | bytes 589828 | tf_op jit(solution)/shard_map/while
  864.2 33.7 %copy-start.14 = (bf16[1,128,12,64]{1,3,2,0:T(8,128)(2,1)S(1)}, bf16[1,128,12,64]{1,3,2,0:T(8,128)(2,1)}, u32[]{:S(2)}) copy-start(bf16[1,128,12,64]{1,3,2,0:T(8,128)(2,1)} %copy-done.13) | copy-start | bytes 589828 | tf_op jit(solution)/shard_map/while
  1011.0 33.7 %copy-start.14 = (bf16[1,128,12,64]{1,3,2,0:T(8,128)(2,1)S(1)}, bf16[1,128,12,64]{1,3,2,0:T(8,128)(2,1)}, u32[]{:S(2)}) copy-start(bf16[1,128,12,64]{1,3,2,0:T(8,128)(2,1)} %copy-done.13) | copy-start | bytes 589828 | tf_op jit(solution)/shard_map/while
  1157.7 33.7 %copy-start.14 = (bf16[1,128,12,64]{1,3,2,0:T(8,128)(2,1)S(1)}, bf16[1,128,12,64]{1,3,2,0:T(8,128)(2,1)}, u32[]{:S(2)}) copy-start(bf16[1,128,12,64]{1,3,2,0:T(8,128)(2,1)} %copy-done.13) | copy-start | bytes 589828 | tf_op jit(solution)/shard_map/while
  1404.2 90.6 %collective-permute-start = (f32[40,768]{1,0:T(8,128)S(1)}, f32[40,768]{1,0:T(8,128)}, u32[]{:S(2)}, u32[]{:S(2)}) collective-permute-start(f32[40,768]{1,0:T(8,128)S(1)} %fusion), channel_id=1, source_target_pairs={{0,1},{1,2},{2,3},{3,4},{4,5},{5,6},{6,7},{7,8},{8,9},{9,10},{10,1... | collective-permute-start | bytes 368648
  1406.1 88.6 %collective-permute-start.1 = (f32[40,768]{1,0:T(8,128)S(1)}, f32[40,768]{1,0:T(8,128)}, u32[]{:S(2)}, u32[]{:S(2)}) collective-permute-start(f32[40,768]{1,0:T(8,128)S(1)} %fusion), channel_id=1, source_target_pairs={{0,2},{1,3},{2,4},{3,5},{4,6},{5,7},{6,8},{7,9},{8,10},{9,11},{10,... | collective-permute-start | bytes 368648
  1408.1 86.7 %collective-permute-start.2 = (f32[40,768]{1,0:T(8,128)S(1)}, f32[40,768]{1,0:T(8,128)}, u32[]{:S(2)}, u32[]{:S(2)}) collective-permute-start(f32[40,768]{1,0:T(8,128)S(1)} %fusion), channel_id=1, source_target_pairs={{0,3},{1,4},{2,5},{3,6},{4,7},{5,8},{6,9},{7,10},{8,11},{9,12},{10... | collective-permute-start | bytes 368648
  1427.2 67.6 %collective-permute-start.3 = (f32[4,768]{1,0:T(4,128)S(1)}, f32[4,768]{1,0:T(4,128)S(1)}, u32[]{:S(2)}, u32[]{:S(2)}) collective-permute-start(f32[4,768]{1,0:T(4,128)S(1)} %slice.362), channel_id=1, source_target_pairs={{0,4},{1,5},{2,6},{3,7},{4,8},{5,9},{6,10},{7,11},{8,12},{9,13},{1... | collective-permute-start | bytes 36872
  (81 other events, 538.9 us)
Sparse Core Ops, SparseCore 0:
  11.5 58.8 all-gather.12
  73.8 58.8 all-gather.6
  136.2 52.8 all-gather.8
  192.4 59.0 all-gather.10
  601.1 97.8 reduce-scatter.8
  706.1 118.0 reduce-scatter.10
  1305.7 133.9 reduce-scatter.6
where the time goes:
time: 1530 us; the launch traced here: 1510 us
  local copies, waits for them, and re-layouts  834 us (55%)
  matrix products  287 us (19%)
  blocking collectives  171 us (11%)
  other arithmetic  139 us (9%)
  waiting for transfers between devices  57.2 us (4%)
    dynamic_update_slice x12, local copies, waits for them, and re-layouts, shards(): lax.map(attend_back, (seq_queries, seq_keys, seq_values, seq_grad_heads,...  257 us
    unnamed x2, blocking collectives  128 us
    slice x64, local copies, waits for them, and re-layouts, widen(): before = jnp.roll(blocked, 1, axis=0)  115 us
    slice x32, local copies, waits for them, and re-layouts, widen(): after = jnp.roll(blocked, -1, axis=0)  76 us
    all_gather x1, waiting for transfers between devices, shards(): lax.all_gather(rounded[0], 'fsdp', axis=0, tiled=True)  57.1 us
    unnamed x103, local copies, waits for them, and re-layouts  54.2 us
    all_gather x1, blocking collectives, shards(): lax.all_gather(rounded[4], 'fsdp', axis=1, tiled=True)  43.1 us
    dot_general x8, matrix products, block_scores(): jnp.einsum('bqhe,bkhe->bhqk', query_blocks, key_wide, preferred_element_t...  42.9 us
  transfers between devices with their start and end apart: 11, of which 1 were waited for; matrix products, arithmetic and copies ran while one was open for 82% of the time, Pallas kernels for 0%

commit v1 on v0

--- a/solution.py
+++ b/solution.py
@@ -18,6 +18,19 @@
 WEIGHT_DECAY = 0.01
 ROPE_BASE = 10000.0
 MASKED = -1e30
+
+
+def view_heaps(t0):
+    placed = jnp.concatenate(
+        jax.lax.all_to_all(
+            jnp.stack([t0 for _ in range(jax.lax.axis_size("fsdp"))]),
+            axis_name="fsdp",
+            split_axis=0,
+            concat_axis=0,
+        ),
+        axis=1,
+    )
+    return placed
 
 
 def layer_norm(values, norm_gain):
@@ -174,7 +187,7 @@
         lax.all_gather(rounded[1], "fsdp", axis=0, tiled=True),
         lax.all_gather(rounded[2], "fsdp", axis=0, tiled=True),
         lax.all_gather(rounded[3], "fsdp", axis=0, tiled=True),
-        lax.all_gather(rounded[4], "fsdp", axis=1, tiled=True),
+        view_heaps(rounded[4]),
     )
     qkv_low, out_low, in_low, down_low, gains_low = gathered
     gains_full = gains_low.astype(jnp.float32)

time: 1530 us -> 1540 us (level)
  blocking collectives: 171 us -> 128 us
  waiting for transfers between devices: 57.2 us -> 91.8 us
    all_gather x1 -> x0, blocking collectives: 43.1 us -> none  [shards(): lax.all_gather(rounded[4], 'fsdp', axis=1, tiled=True)]
    all_gather x1, waiting for transfers between devices: 0.01 us -> 32.9 us  [shards(): lax.all_gather(rounded[3], 'fsdp', axis=0, tiled=True)]
    unnamed x103 -> x101, local copies, waits for them, and re-layouts: 54.2 us -> 57.7 us
  transfers between devices with their start and end apart: 11 -> 12, of which waited for: 1 -> 2; matrix products, arithmetic and copies ran while one was open for 82% -> 82% of each run, Pallas kernels for 0% -> 0%
where the time goes in v1:
time: 1540 us; the launch traced here: 1520 us
  local copies, waits for them, and re-layouts  838 us (54%)
  matrix products  289 us (19%)
  other arithmetic  140 us (9%)
  blocking collectives  128 us (8%)
  waiting for transfers between devices  91.8 us (6%)
    dynamic_update_slice x12, local copies, waits for them, and re-layouts, shards(): lax.map(attend_back, (seq_queries, seq_keys, seq_values, seq_grad_heads,...  257 us
    unnamed x2, blocking collectives  128 us
    slice x64, local copies, waits for them, and re-layouts, widen(): before = jnp.roll(blocked, 1, axis=0)  115 us
    slice x32, local copies, waits for them, and re-layouts, widen(): after = jnp.roll(blocked, -1, axis=0)  75.6 us
    all_gather x1, waiting for transfers between devices, shards(): lax.all_gather(rounded[0], 'fsdp', axis=0, tiled=True)  58.7 us
    unnamed x101, local copies, waits for them, and re-layouts  57.7 us
    dot_general x8, matrix products, block_scores(): jnp.einsum('bqhe,bkhe->bhqk', query_blocks, key_wide, preferred_element_t...  43 us
    reshape x16, local copies, waits for them, and re-layouts, block_scores(): key_wide = widen(key_heads.reshape(block_count, BLK, HEADS, HEAD))  37.3 us
  transfers between devices with their start and end apart: 12, of which 2 were waited for; matrix products, arithmetic and copies ran while one was open for 82% of the time, Pallas kernels for 0%

profile of v1, /device:TPU:0, one launch (start us, length us, event | category | flops | bytes accessed | tf_op | source)
XLA Modules:
  0.0 1518.3 jit_solution(11908365666583091359)
XLA Ops:
  37.4 32.9 %all-gather.12.cloned.1.call-done = bf16[32,36,768]{2,1,0:T(8,128)(2,1)} async-done(((bf16[1,36,768]{2,1,0:T(8,128)(2,1)}), bf16[32,36,768]{2,1,0:T(8,128)(2,1)}) %all-gather.12.cloned.1.call-update) | async-done | bytes 1769488 | tf_op jit(solution)/shard_map/all_gather | solution.py:189
  74.0 58.7 %all-gather.6.cloned.1.call-done = bf16[768,2304]{1,0:T(8,128)(2,1)} async-done(((bf16[24,2304]{1,0:T(8,128)(2,1)}), bf16[768,2304]{1,0:T(8,128)(2,1)}) %all-gather.6.cloned.1.call-update) | async-done | bytes 3538960 | tf_op jit(solution)/shard_map/all_gather | solution.py:186
  132.7 13.7 fusion.103
  224.0 10.3 fusion.94
  250.8 250.6 %while.30 = (s32[]{:T(128)}, bf16[4,512,12,64]{1,3,2,0:T(8,128)(2,1)}, f32[4,4,12,128,1]{3,2,1,4,0:T(8,128)}, bf16[4,512,12,64]{1,3,2,0:T(8,128)(2,1)S(1)}, s32[...) while((s32[]{:T(128)}, ...), condition=%wide.region_5.6_spmd, body=%wide.region_2.5_spmd.sunk | while | flops 657465344 | bytes 106623328 | solution.py:212
  519.1 11.3 fusion.121
  530.4 26.1 %fusion.98 = (f32[2048,1152]{1,0:T(8,128)}, f32[2048,1152]{1,0:T(8,128)}, f32[2048,1152]{1,0:T(8,128)}) fusion(f32[2048,2304]{1,0:T(8,128)S(1)} %fusion.121, bf16[2048,768]{1,0:T(8,128)(2,1)S(1)} %copy-done.19, bf16[1152,768]{1,0:T(8,128)(2,1)S(1)} %copy-done.26), kind=kOutput, calls=%fused_computation.188 | convolution fusion | flops 3777232896 | bytes 42663936 | tf_op jit(solution)/shard_map/dot_general | solution.py:231
  556.5 14.6 multiply_add_fusion
  571.1 16.3 %multiply_reduce_fusion.1 = (f32[768]{0:T(1024)}, f32[2048]{0:T(1024)S(1)}, f32[2048,768]{0,1:T(8,128)}) fusion(f32[2048,768]{0,1:T(8,128)} %copy-done.10, f32[2048]{0:T(1024)S(1)} %fusion.115, f32[2048]{0:T(1024)S(1)} %broadcast_multiply_fusion.2, f32[768]{0:T(1024)S(1)} %copy-done.42, bf16[768,2304]{1,0:T(8,128)(2,1)} %all-gather.10.cloned.1.call-done, ...), kind=kOutput, calls=%fused_computation.173 | convolution fusion | flops 7268201472 | bytes 35026944 | tf_op jit(solution)/shard_map/dot_general | solution.py:234
  623.1 19.0 %fusion.99 = f32[768,2304]{1,0:T(8,128)} fusion(f32[2048,1152]{1,0:T(8,128)} %get-tuple-element.476, f32[2048,1152]{1,0:T(8,128)} %get-tuple-element.424, f32[2048,768]{0,1:T(8,128)} %copy-done.10, f32[768]{0:T(1024)S(1)} %copy-done.42, f32[2048]{0:T(1024)S(1)} %fusion.115, f32[2048]{0:T(1024)S(1)} %broadcast_multiply_fusion.2), kind=kOutput, calls=%fused_computation.189 | convolution fusion | flops 7263485952 | bytes 32263168 | tf_op jit(solution)/shard_map/dot_general | solution.py:233
  644.0 588.6 %while.31 = (s32[]{:T(128)}, f32[4,512,12,64]{1,0,3,2:T(4,128)}, f32[4,512,12,64]{1,0,3,2:T(4,128)}, bf16[4,512,12,64]{1,3,2,0:T(8,128)(2,1)}, bf16[4,512,12,64]...) while((s32[]{:T(128)}, f32[4,512,12,64]{1,0,3,2:T(4,128)}, ...), condition=%wide.region_12.13_spmd, body=%wide.region_10.12_spmd.sunk | while | flops 1587027968 | bytes 218263584 | solution.py:243
  721.9 31.2 %dynamic_update_slice.45 = f32[4,512,12,64]{1,0,3,2:T(4,128)} dynamic-update-slice(f32[4,512,12,64]{1,0,3,2:T(4,128)} %get-tuple-element.751, f32[1,512,12,64]{1,0,3,2:T(1,128)} %bitcast.200, s32[]{:T(128)} %get-tuple-element.749, s32[]{:T(128)} %constant.218.clone.1..sunk.1, s32[]{:T(128)} %constant.218.clone.1..sunk.1, s32[]{:T(128)} %constant.218.clone.1..sunk.1) | dynamic-update-slice | bytes 3145732 | tf_op jit(solution)/shard_map/while/body/jit(dynamic_update_index_in_dim)/dynamic_update_slice | solution.py:243
  760.5 31.1 %dynamic_update_slice.44 = f32[4,512,12,64]{1,0,3,2:T(4,128)} dynamic-update-slice(f32[4,512,12,64]{1,0,3,2:T(4,128)} %get-tuple-element.750, f32[1,512,12,64]{1,0,3,2:T(1,128)} %bitcast.199, s32[]{:T(128)} %get-tuple-element.749, s32[]{:T(128)} %constant.218.clone.1..sunk.1, s32[]{:T(128)} %constant.218.clone.1..sunk.1, s32[]{:T(128)} %constant.218.clone.1..sunk.1) | dynamic-update-slice | bytes 3145732 | tf_op jit(solution)/shard_map/while/body/jit(dynamic_update_index_in_dim)/dynamic_update_slice | solution.py:243
  869.2 31.0 %dynamic_update_slice.45 = f32[4,512,12,64]{1,0,3,2:T(4,128)} dynamic-update-slice(f32[4,512,12,64]{1,0,3,2:T(4,128)} %get-tuple-element.751, f32[1,512,12,64]{1,0,3,2:T(1,128)} %bitcast.200, s32[]{:T(128)} %get-tuple-element.749, s32[]{:T(128)} %constant.218.clone.1..sunk.1, s32[]{:T(128)} %constant.218.clone.1..sunk.1, s32[]{:T(128)} %constant.218.clone.1..sunk.1) | dynamic-update-slice | bytes 3145732 | tf_op jit(solution)/shard_map/while/body/jit(dynamic_update_index_in_dim)/dynamic_update_slice | solution.py:243
  907.5 31.0 %dynamic_update_slice.44 = f32[4,512,12,64]{1,0,3,2:T(4,128)} dynamic-update-slice(f32[4,512,12,64]{1,0,3,2:T(4,128)} %get-tuple-element.750, f32[1,512,12,64]{1,0,3,2:T(1,128)} %bitcast.199, s32[]{:T(128)} %get-tuple-element.749, s32[]{:T(128)} %constant.218.clone.1..sunk.1, s32[]{:T(128)} %constant.218.clone.1..sunk.1, s32[]{:T(128)} %constant.218.clone.1..sunk.1) | dynamic-update-slice | bytes 3145732 | tf_op jit(solution)/shard_map/while/body/jit(dynamic_update_index_in_dim)/dynamic_update_slice | solution.py:243
  1016.0 31.0 %dynamic_update_slice.45 = f32[4,512,12,64]{1,0,3,2:T(4,128)} dynamic-update-slice(f32[4,512,12,64]{1,0,3,2:T(4,128)} %get-tuple-element.751, f32[1,512,12,64]{1,0,3,2:T(1,128)} %bitcast.200, s32[]{:T(128)} %get-tuple-element.749, s32[]{:T(128)} %constant.218.clone.1..sunk.1, s32[]{:T(128)} %constant.218.clone.1..sunk.1, s32[]{:T(128)} %constant.218.clone.1..sunk.1) | dynamic-update-slice | bytes 3145732 | tf_op jit(solution)/shard_map/while/body/jit(dynamic_update_index_in_dim)/dynamic_update_slice | solution.py:243
  1054.4 31.0 %dynamic_update_slice.44 = f32[4,512,12,64]{1,0,3,2:T(4,128)} dynamic-update-slice(f32[4,512,12,64]{1,0,3,2:T(4,128)} %get-tuple-element.750, f32[1,512,12,64]{1,0,3,2:T(1,128)} %bitcast.199, s32[]{:T(128)} %get-tuple-element.749, s32[]{:T(128)} %constant.218.clone.1..sunk.1, s32[]{:T(128)} %constant.218.clone.1..sunk.1, s32[]{:T(128)} %constant.218.clone.1..sunk.1) | dynamic-update-slice | bytes 3145732 | tf_op jit(solution)/shard_map/while/body/jit(dynamic_update_index_in_dim)/dynamic_update_slice | solution.py:243
  1162.9 31.0 %dynamic_update_slice.45 = f32[4,512,12,64]{1,0,3,2:T(4,128)} dynamic-update-slice(f32[4,512,12,64]{1,0,3,2:T(4,128)} %get-tuple-element.751, f32[1,512,12,64]{1,0,3,2:T(1,128)} %bitcast.200, s32[]{:T(128)} %get-tuple-element.749, s32[]{:T(128)} %constant.218.clone.1..sunk.1, s32[]{:T(128)} %constant.218.clone.1..sunk.1, s32[]{:T(128)} %constant.218.clone.1..sunk.1) | dynamic-update-slice | bytes 3145732 | tf_op jit(solution)/shard_map/while/body/jit(dynamic_update_index_in_dim)/dynamic_update_slice | solution.py:243
  1201.2 31.0 %dynamic_update_slice.44 = f32[4,512,12,64]{1,0,3,2:T(4,128)} dynamic-update-slice(f32[4,512,12,64]{1,0,3,2:T(4,128)} %get-tuple-element.750, f32[1,512,12,64]{1,0,3,2:T(1,128)} %bitcast.199, s32[]{:T(128)} %get-tuple-element.749, s32[]{:T(128)} %constant.218.clone.1..sunk.1, s32[]{:T(128)} %constant.218.clone.1..sunk.1, s32[]{:T(128)} %constant.218.clone.1..sunk.1) | dynamic-update-slice | bytes 3145732 | tf_op jit(solution)/shard_map/while/body/jit(dynamic_update_index_in_dim)/dynamic_update_slice | solution.py:243
  1296.8 14.2 fusion.96
  1320.1 89.3 %fusion = f32[40,768]{1,0:T(8,128)S(1)} fusion(f32[1152,768]{1,0:T(8,128)} %fusion.138), kind=kCustom, calls=%all-reduce-scatter | all-reduce-scatter fusion | flops 983041 | bytes 3661824
  1415.2 11.3 fusion.86
  1433.7 38.5 %all-reduce.3 = f32[2,768]{1,0:T(2,128)S(1)} all-reduce(f32[2,768]{1,0:T(2,128)S(1)} %pad_maximum_fusion.5), channel_id=6, replica_groups=mesh['fsdp'=32] {'fsdp'}, use_global_device_ids=true, to_apply=%region_21.22.clone | all-reduce | flops 1536 | bytes 12288
  1472.3 10.8 add_convert_fusion.1
  (620 shorter events, 885.2 us)
Async XLA Ops:
  7.2 63.2 %all-gather.12.cloned.1.call-start = ((), (), s32[]{:S(2)}) async-start(), calls=%async_computation.10 | async-start | bytes 2027520 | tf_op jit(solution)/shard_map/all_gather | solution.py:189
  8.8 123.9 %all-gather.6.cloned.1.call-start = ((), (), s32[]{:S(2)}) async-start(), calls=%async_computation.4 | async-start | bytes 3649536 | tf_op jit(solution)/shard_map/all_gather | solution.py:186
  10.5 499.1 %all-gather.8.cloned.1.call-start = ((), (), s32[]{:S(2)}) async-start(), calls=%async_computation.5 | async-start | bytes 1216512 | tf_op jit(solution)/shard_map/all_gather | solution.py:187
  13.3 23.2 %all-to-all-start = ((bf16[32,2,24]{2,1,0:T(2,128)(2,1)}), bf16[32,2,24]{2,1,0:T(2,128)(2,1)S(1)}, u32[]{:S(2)}, u32[]{:S(2)}) async-start(bf16[32,2,24]{2,1,0:T(2,128)(2,1)} %stack.4), calls=%async_computation | async-start | bytes 32768 | tf_op jit(solution)/shard_map/all_to_all | solution.py:25
  20.7 498.4 %all-gather.10.cloned.1.call-start = ((), (), s32[]{:S(2)}) async-start(), calls=%async_computation.6 | async-start | bytes 3649536 | tf_op jit(solution)/shard_map/all_gather | solution.py:188
  22.3 1482.7 %reduce-scatter.9.cloned.1.call-start = ((), (), s32[]{:S(2)}) async-start(), calls=%async_computation.8 | async-start | bytes 2433024 | tf_op jit(solution)/shard_map/reduce_scatter | solution.py:263
  25.6 107.1 %copy-start.5 = (bf16[2048,768]{0,1:T(8,128)(2,1)}, bf16[2048,768]{0,1:T(8,128)(2,1)S(1)}, u32[]{:S(2)}) copy-start(bf16[2048,768]{0,1:T(8,128)(2,1)S(1)} %copy.124) | copy-start | bytes 9437188
  26.1 106.6 %copy-start.30 = (f32[2048]{0:T(1024)}, f32[2048]{0:T(1024)S(1)}, u32[]{:S(2)}) copy-start(f32[2048]{0:T(1024)S(1)} %broadcast_multiply_fusion.3) | copy-start | bytes 24580
  27.0 119.4 %copy-start.32 = (f32[2048]{0:T(1024)}, f32[2048]{0:T(1024)S(1)}, u32[]{:S(2)}) copy-start(f32[2048]{0:T(1024)S(1)} %fusion.114) | copy-start | bytes 24580
  36.7 109.7 %copy-start.40 = (f32[768]{0:T(1024)}, f32[768]{0:T(1024)S(1)}, u32[]{:S(2)}) copy-start(f32[768]{0:T(1024)S(1)} %mul.471) | copy-start | bytes 9220
  602.1 904.7 %reduce-scatter.11.cloned.1.call-start = ((), (), s32[]{:S(2)}) async-start(), calls=%async_computation.9 | async-start | bytes 7299072 | tf_op jit(solution)/shard_map/reduce_scatter | solution.py:264
  642.1 866.7 %reduce-scatter.7.cloned.1.call-start = ((), (), s32[]{:S(2)}) async-start(), calls=%async_computation.7 | async-start | bytes 7299072 | tf_op jit(solution)/shard_map/reduce_scatter | solution.py:262
  658.4 16.9 %copy-start.13 = (bf16[1,128,12,64]{1,3,2,0:T(8,128)(2,1)}, bf16[1,128,12,64]{1,3,2,0:T(8,128)(2,1)S(1)}, u32[]{:S(2)}) copy-start(bf16[1,128,12,64]{1,3,2,0:T(8,128)(2,1)S(1)} %get-tuple-element.675) | copy-start | bytes 589828 | tf_op jit(solution)/shard_map/while
  719.3 33.9 %copy-start.14 = (bf16[1,128,12,64]{1,3,2,0:T(8,128)(2,1)S(1)}, bf16[1,128,12,64]{1,3,2,0:T(8,128)(2,1)}, u32[]{:S(2)}) copy-start(bf16[1,128,12,64]{1,3,2,0:T(8,128)(2,1)} %copy-done.13) | copy-start | bytes 589828 | tf_op jit(solution)/shard_map/while
  805.8 16.8 %copy-start.13 = (bf16[1,128,12,64]{1,3,2,0:T(8,128)(2,1)}, bf16[1,128,12,64]{1,3,2,0:T(8,128)(2,1)S(1)}, u32[]{:S(2)}) copy-start(bf16[1,128,12,64]{1,3,2,0:T(8,128)(2,1)S(1)} %get-tuple-element.675) | copy-start | bytes 589828 | tf_op jit(solution)/shard_map/while
  866.5 33.7 %copy-start.14 = (bf16[1,128,12,64]{1,3,2,0:T(8,128)(2,1)S(1)}, bf16[1,128,12,64]{1,3,2,0:T(8,128)(2,1)}, u32[]{:S(2)}) copy-start(bf16[1,128,12,64]{1,3,2,0:T(8,128)(2,1)} %copy-done.13) | copy-start | bytes 589828 | tf_op jit(solution)/shard_map/while
  952.8 16.7 %copy-start.13 = (bf16[1,128,12,64]{1,3,2,0:T(8,128)(2,1)}, bf16[1,128,12,64]{1,3,2,0:T(8,128)(2,1)S(1)}, u32[]{:S(2)}) copy-start(bf16[1,128,12,64]{1,3,2,0:T(8,128)(2,1)S(1)} %get-tuple-element.675) | copy-start | bytes 589828 | tf_op jit(solution)/shard_map/while
  1013.4 33.7 %copy-start.14 = (bf16[1,128,12,64]{1,3,2,0:T(8,128)(2,1)S(1)}, bf16[1,128,12,64]{1,3,2,0:T(8,128)(2,1)}, u32[]{:S(2)}) copy-start(bf16[1,128,12,64]{1,3,2,0:T(8,128)(2,1)} %copy-done.13) | copy-start | bytes 589828 | tf_op jit(solution)/shard_map/while
  1099.6 16.7 %copy-start.13 = (bf16[1,128,12,64]{1,3,2,0:T(8,128)(2,1)}, bf16[1,128,12,64]{1,3,2,0:T(8,128)(2,1)S(1)}, u32[]{:S(2)}) copy-start(bf16[1,128,12,64]{1,3,2,0:T(8,128)(2,1)S(1)} %get-tuple-element.675) | copy-start | bytes 589828 | tf_op jit(solution)/shard_map/while
  1160.2 33.7 %copy-start.14 = (bf16[1,128,12,64]{1,3,2,0:T(8,128)(2,1)S(1)}, bf16[1,128,12,64]{1,3,2,0:T(8,128)(2,1)}, u32[]{:S(2)}) copy-start(bf16[1,128,12,64]{1,3,2,0:T(8,128)(2,1)} %copy-done.13) | copy-start | bytes 589828 | tf_op jit(solution)/shard_map/while
  1409.4 90.6 %collective-permute-start = (f32[40,768]{1,0:T(8,128)S(1)}, f32[40,768]{1,0:T(8,128)}, u32[]{:S(2)}, u32[]{:S(2)}) collective-permute-start(f32[40,768]{1,0:T(8,128)S(1)} %fusion), channel_id=1, source_target_pairs={{0,1},{1,2},{2,3},{3,4},{4,5},{5,6},{6,7},{7,8},{8,9},{9,10},{10,1... | collective-permute-start | bytes 368648
  1411.4 88.6 %collective-permute-start.1 = (f32[40,768]{1,0:T(8,128)S(1)}, f32[40,768]{1,0:T(8,128)}, u32[]{:S(2)}, u32[]{:S(2)}) collective-permute-start(f32[40,768]{1,0:T(8,128)S(1)} %fusion), channel_id=1, source_target_pairs={{0,2},{1,3},{2,4},{3,5},{4,6},{5,7},{6,8},{7,9},{8,10},{9,11},{10,... | collective-permute-start | bytes 368648
  1413.3 86.7 %collective-permute-start.2 = (f32[40,768]{1,0:T(8,128)S(1)}, f32[40,768]{1,0:T(8,128)}, u32[]{:S(2)}, u32[]{:S(2)}) collective-permute-start(f32[40,768]{1,0:T(8,128)S(1)} %fusion), channel_id=1, source_target_pairs={{0,3},{1,4},{2,5},{3,6},{4,7},{5,8},{6,9},{7,10},{8,11},{9,12},{10... | collective-permute-start | bytes 368648
  1432.4 67.6 %collective-permute-start.3 = (f32[4,768]{1,0:T(4,128)S(1)}, f32[4,768]{1,0:T(4,128)S(1)}, u32[]{:S(2)}, u32[]{:S(2)}) collective-permute-start(f32[4,768]{1,0:T(4,128)S(1)} %slice.364), channel_id=1, source_target_pairs={{0,4},{1,5},{2,6},{3,7},{4,8},{5,9},{6,10},{7,11},{8,12},{9,13},{1... | collective-permute-start | bytes 36872
  (81 other events, 492.8 us)
Sparse Core Ops, SparseCore 0:
  11.5 58.8 all-gather.11
  73.8 58.8 all-gather.5
  136.2 52.8 all-gather.7
  192.4 58.9 all-gather.9
  602.2 97.9 reduce-scatter.8
  707.2 118.1 reduce-scatter.10
  1311.2 133.5 reduce-scatter.6
